TPU v7x, 32 devices: a whole 2x2x4 slice. The times are simulated.
32 devices in a mesh: groups: 2 (over y), seq: 4 (over z), help: 2 (over x), head: 2 (over core).
Axes of the slice: x: 2, y: 2, z: 4, core: 2. Of those that a mesh axis runs over, the one named last changes fastest.
Arguments:
- query_rows: bfloat16 [2048, 2048], P(('groups', 'seq', 'help'), 'head'), parts along dimension 0, may hold values from -5.5 to 5.5
- key_rows: bfloat16 [2048, 2048], P(('groups', 'seq', 'help'), 'head'), parts along dimension 0, may hold values from -5.5 to 5.5
- value_rows: bfloat16 [2048, 2048], P(('groups', 'seq', 'help'), 'head'), parts along dimension 0, may hold values from -6 to 6
- out_grad: bfloat16 [2048, 2048], P(('groups', 'seq', 'help'), 'head'), parts along dimension 0, may hold values from -6 to 6
- cluster_ids: int32 [16, 2048, 1], P('head', ('groups', 'seq', 'help')), parts along dimension 1, may hold values from 0 to 127; in each aligned block of 128 rows (0 to 127, 128 to 255, ..., all dimensions but the last counted through in order) at most 2 rows name the same one
- cluster_slots: int32 [32, 128], P(('groups', 'head')), parts along dimension 0, may hold values from 0 to 127, each once within a row
Outputs:
- attended: bfloat16 [2048, 2048], P(('groups', 'seq', 'help'), 'head'), parts along dimension 0
- grad_queries: bfloat16 [2048, 2048], P(('groups', 'seq', 'help'), 'head'), parts along dimension 0
- grad_keys: bfloat16 [2048, 2048], P(('groups', 'seq', 'help'), 'head'), parts along dimension 0
- grad_values: bfloat16 [2048, 2048], P(('groups', 'seq', 'help'), 'head'), parts along dimension 0
- centroid_sums: float32 [32, 128, 128], P(('groups', 'head'), ('seq', 'help')), parts along dimension 0
There are 2 independent parts, one for each index of `groups`. A program takes and returns all parts, laid end to end along the dimension named above; each array names one. Nothing has to cross between parts.
Inputs may be any that keep to these rules, and one draw needn't show every extreme that they name: `cluster_ids`: in each aligned block of 128 rows (one head's tokens on one device) no cluster is named more than 2 times, a bound that some block reaches. `cluster_slots`: each head's row names every slot once.
All inputs are finite; a program needn't handle non-finite values.
Results may differ from a plain program's by a relative error of at most 0.0062.
Values may be sent and summed in bfloat16 or wider, within the bound.
A program may use at most 64 MiB of HBM per device.

v0:
```python
import jax
import jax.numpy as jnp
from jax import lax
from jax.sharding import PartitionSpec as P

BLK = 256
MOST = 2


def unit_keys(key_part):
    key_float = key_part.astype(jnp.float32)
    spread = jnp.mean(key_float * key_float, axis=-1, keepdims=True)
    return key_float * lax.rsqrt(spread + 1e-06) * key_part.shape[-1] ** (-0.5)


def cluster_attention(packed_rows, token_pos):
    depth = packed_rows.shape[-1] // 4
    count = packed_rows.shape[0]
    query_part = packed_rows[:, :depth]
    key_part = packed_rows[:, depth : 2 * depth]
    value_part = packed_rows[:, 2 * depth : 3 * depth]
    grad_part = packed_rows[:, 3 * depth :]
    valid = token_pos >= 0
    rank = jnp.cumsum(valid.astype(jnp.int32)) - 1
    block_id = rank // BLK
    allowed = valid[:, None] & valid[None, :] & (block_id[:, None] == block_id[None, :])
    allowed = allowed & (token_pos[None, :] <= token_pos[:, None])
    allowed = allowed | jnp.eye(count, dtype=bool)
    scale = depth ** (-0.5)
    scores = (
        lax.dot_general(
            query_part, key_part, (((1,), (1,)), ((), ())), preferred_element_type=jnp.float32
        )
        * scale
    )
    scores = jnp.where(allowed, scores, -1e30)
    peak = jnp.max(scores, axis=1, keepdims=True)
    weights = jnp.exp(scores - peak)
    weights = weights / jnp.sum(weights, axis=1, keepdims=True)
    weights_low = weights.astype(jnp.bfloat16)
    context = jnp.dot(weights_low, value_part, preferred_element_type=jnp.float32)
    grad_value = lax.dot_general(
        weights_low, grad_part, (((0,), (0,)), ((), ())), preferred_element_type=jnp.float32
    )
    grad_weights = lax.dot_general(
        grad_part, value_part, (((1,), (1,)), ((), ())), preferred_element_type=jnp.float32
    )
    delta = jnp.sum(grad_part.astype(jnp.float32) * context, axis=1, keepdims=True)
    grad_scores = (weights * (grad_weights - delta)).astype(jnp.bfloat16)
    grad_query = jnp.dot(grad_scores, key_part, preferred_element_type=jnp.float32) * scale
    grad_key = (
        lax.dot_general(
            grad_scores, query_part, (((0,), (0,)), ((), ())), preferred_element_type=jnp.float32
        )
        * scale
    )
    return jnp.concatenate([context, grad_query, grad_key, grad_value], axis=1).astype(jnp.bfloat16)


def owner_work(arrived, arrived_pos):
    head_count, per_device, source_count, most_count, packed_width = arrived.shape
    flat_rows = arrived.reshape(head_count, per_device, source_count * most_count, packed_width)
    flat_pos = arrived_pos.reshape(head_count, per_device, source_count * most_count)

    def one_head(head_pair):
        return jax.vmap(cluster_attention)(head_pair[0], head_pair[1])

    results = lax.map(one_head, (flat_rows, flat_pos)).reshape(arrived.shape)
    owner_sums = jnp.zeros((head_count, 1), jnp.float32)
    return (results, owner_sums)


def local(query_rows, key_rows, value_rows, out_grad, cluster_ids, cluster_slots):
    token_count, width = query_rows.shape
    local_heads, cluster_total = cluster_slots.shape
    depth = width // local_heads
    seq_size = lax.axis_size("seq")
    help_size = lax.axis_size("help")
    device_count = seq_size * help_size
    per_device = cluster_total // device_count
    packed = jnp.concatenate(
        [
            piece.reshape(token_count, local_heads, depth)
            for piece in (query_rows, key_rows, value_rows, out_grad)
        ],
        axis=2,
    )
    packed = packed.transpose(1, 0, 2)
    labels = cluster_ids[:, :, 0]
    matches = labels[:, :, None] == jnp.arange(cluster_total, dtype=jnp.int32)[None, None, :]
    slot_of = jnp.sum(jnp.where(matches, cluster_slots[:, None, :], 0), axis=2)
    positions = jnp.arange(token_count, dtype=jnp.int32)
    earlier = (labels[:, :, None] == labels[:, None, :]) & (
        positions[None, None, :] < positions[None, :, None]
    )
    within = jnp.sum(earlier.astype(jnp.int32), axis=2)
    target = slot_of // per_device
    column = slot_of % per_device
    flat_slot = (column * device_count + target) * MOST + within
    slot_total = per_device * device_count * MOST
    head_index = jnp.arange(local_heads, dtype=jnp.int32)[:, None]
    send_rows = (
        jnp.zeros((local_heads, slot_total, 4 * depth), jnp.bfloat16)
        .at[head_index, flat_slot]
        .set(packed)
    )
    global_pos = lax.axis_index(("seq", "help")) * token_count + positions
    send_pos = (
        jnp.full((local_heads, slot_total), -1, jnp.int32)
        .at[head_index, flat_slot]
        .set(jnp.broadcast_to(global_pos, (local_heads, token_count)))
    )
    grid_rows = (local_heads, per_device, device_count, MOST, 4 * depth)
    results, owner_sums = owner_work(
        lax.all_to_all(
            send_rows.reshape(grid_rows), ("seq", "help"), split_axis=2, concat_axis=2, tiled=True
        ),
        lax.all_to_all(
            send_pos.reshape(grid_rows[:-1]),
            ("seq", "help"),
            split_axis=2,
            concat_axis=2,
            tiled=True,
        ),
    )
    returned, owner_sums = (
        lax.all_to_all(results, ("seq", "help"), split_axis=2, concat_axis=2, tiled=True),
        owner_sums,
    )
    gathered = returned.reshape(local_heads, slot_total, 4 * depth)[head_index, flat_slot]
    gathered = gathered.transpose(1, 0, 2)
    pieces = [
        gathered[:, :, index * depth : (index + 1) * depth].reshape(token_count, width)
        for index in range(4)
    ]
    units = unit_keys(packed[:, :, depth : 2 * depth])
    chosen = (
        slot_of[:, :, None]
        == jnp.arange(lax.axis_size(("seq", "help")) * per_device, dtype=jnp.int32)[None, None, :]
    )
    centroid_sums = lax.psum_scatter(
        jnp.einsum(
            "htc,htd->chd", chosen.astype(jnp.float32), units, precision=lax.Precision.HIGHEST
        ),
        ("seq", "help"),
        scatter_dimension=0,
        tiled=True,
    ).transpose(1, 0, 2)
    return (pieces[0], pieces[1], pieces[2], pieces[3], centroid_sums)


def solution(mesh):
    in_specs = (
        P(("groups", "seq", "help"), "head"),
        P(("groups", "seq", "help"), "head"),
        P(("groups", "seq", "help"), "head"),
        P(("groups", "seq", "help"), "head"),
        P("head", ("groups", "seq", "help"), None),
        P(("groups", "head"), None),
    )
    out_specs = (
        P(("groups", "seq", "help"), "head"),
        P(("groups", "seq", "help"), "head"),
        P(("groups", "seq", "help"), "head"),
        P(("groups", "seq", "help"), "head"),
        P(("groups", "head"), ("seq", "help"), None),
    )
    return jax.shard_map(local, mesh=mesh, in_specs=in_specs, out_specs=out_specs, check_vma=False)
```

profile of v0, /device:TPU:0, one launch (start us, length us, event | category | flops | bytes accessed | tf_op | source)
XLA Modules:
  0.0 243.2 jit_solution(7113388861293958497)
XLA Ops:
  7.2 1.3 select_reduce_fusion
  8.5 0.7 and_reduce_fusion
  9.3 0.7 multiply_reduce_fusion.1
  10.0 4.3 %scatter_custom_fusion = s32[2048]{0:T(1024)S(1)} fusion(s32[1024]{0:T(1024)S(1)} %get-tuple-element.148, s32[1024]{0:T(1024)S(1)} %get-tuple-element.149, s32[]{:T(128)} %constant.134.clone.1), kind=kCustom, calls=%fused_computation.88 | custom fusion | bytes 8196
  14.3 0.5 reshape.313
  14.8 0.5 copy.91
  15.3 0.7 reshape.359
  16.0 7.3 %all-to-all-start = ((s32[8,1,256]{2,1,0:T(1,128)}), s32[8,1,256]{2,1,0:T(1,128)S(1)}, u32[]{:S(2)}, u32[]{:S(2)}) async-start(s32[8,1,256]{2,1,0:T(1,128)} %reshape.359), calls=%async_computation | async-start | bytes 16384 | tf_op jit(solution)/shard_map/all_to_all | solution.py:118
  23.2 1.1 copy.92
  24.3 1.1 copy.93
  25.9 1.3 copy.96
  27.3 6.3 %scatter_custom_fusion.1 = bf16[2048,512]{1,0:T(8,128)(2,1)S(1)} fusion(s32[1024]{0:T(1024)S(1)} %get-tuple-element.148, bf16[1024,512]{1,0:T(8,128)(2,1)} %bitcast.112, bf16[]{:T(256)} %constant.128.clone.1), kind=kCustom, calls=%fused_computation.48 | custom fusion | bytes 2097664
  33.5 2.2 reshape.319
  35.8 5.2 %copy.97 = bf16[8,16,8,2,512]{4,3,1,0,2:T(2,128)(2,1)} copy(bf16[8,16,8,2,512]{4,3,2,1,0:T(2,128)(2,1)} %reshape.319) | data formatting | bytes 4194304 | tf_op jit(solution)/shard_map/reshape | solution.py:116
  41.0 6.0 %all-to-all-start.1 = ((bf16[8,16,8,2,512]{4,3,1,0,2:T(2,128)(2,1)}), bf16[8,16,8,2,512]{4,3,1,0,2:T(2,128)(2,1)S(1)}, u32[]{:S(2)}, u32[]{:S(2)}) async-start(bf16[8,16,8,2,512]{4,3,1,0,2:T(2,128)(2,1)} %copy.97), calls=%async_computation.1 | async-start | bytes 4194304 | tf_op jit(solution)/shard_map/all_to_all | solution.py:115
  47.0 0.5 broadcast.338
  47.5 0.7 reduce.6
  48.3 46.4 %all-to-all-done.1 = bf16[8,16,8,2,512]{4,3,1,0,2:T(2,128)(2,1)S(1)} async-done(((bf16[8,16,8,2,512]{4,3,1,0,2:T(2,128)(2,1)}), bf16[8,16,8,2,512]{4,3,1,0,2:T(2,128)(2,1)S(1)}, u32[]{:S(2)}, u32[]{:S(2)}) %all-to-all-start.1) | async-done | bytes 2097184 | tf_op jit(solution)/shard_map/all_to_all | solution.py:115
  94.7 1.9 copy.98
  96.6 28.8 %while.13 = (s32[]{:T(128)}, bf16[8,16,16,512]{3,1,2,0:T(8,128)(2,1)}, s32[8,16,16]{1,0,2:T(8,128)S(1)}, bf16[8,16,16,512]{3,1,2,0:T(8,128)(2,1)}, s32[]{:T(128)}, /*index=5*/s32[]{:T(128)}) while((s32[]{:T(128)}, bf16[8,16,16,512]{3,1,2,0:T(8,128)(2,1)}, s32[8,16,16]{1,0,2:T(8,128)S(1)}, bf16[8,16,16,512]{3,1,2,0:T(8,128)(2,1)}, s32[]{:T(128)}, ...), condition=%wide.region_9.10_spmd, body=%wide.region_4.9_spmd.sunk | while | flops 7717137 | bytes 3582557 | solution.py:68
  96.9 1.0 constant_dynamic-slice_fusion.4
  98.0 0.2 fusion.89
  98.4 0.3 convert_bitcast_fusion.2
  99.3 0.9 copy_dynamic-update-slice_fusion.2
  100.5 1.0 constant_dynamic-slice_fusion.4
  101.6 0.2 fusion.89
  102.0 0.3 convert_bitcast_fusion.2
  103.0 0.9 copy_dynamic-update-slice_fusion.2
  104.1 1.0 constant_dynamic-slice_fusion.4
  105.2 0.2 fusion.89
  105.6 0.3 convert_bitcast_fusion.2
  106.6 0.9 copy_dynamic-update-slice_fusion.2
  107.7 1.0 constant_dynamic-slice_fusion.4
  108.8 0.2 fusion.89
  109.2 0.3 convert_bitcast_fusion.2
  110.1 0.9 copy_dynamic-update-slice_fusion.2
  111.3 1.0 constant_dynamic-slice_fusion.4
  112.4 0.2 fusion.89
  112.8 0.3 convert_bitcast_fusion.2
  113.8 0.9 copy_dynamic-update-slice_fusion.2
  114.9 1.0 constant_dynamic-slice_fusion.4
  116.5 0.3 convert_bitcast_fusion.2
  117.4 0.9 copy_dynamic-update-slice_fusion.2
  118.5 1.0 constant_dynamic-slice_fusion.4
  120.1 0.3 convert_bitcast_fusion.2
  121.0 0.9 copy_dynamic-update-slice_fusion.2
  122.1 1.0 constant_dynamic-slice_fusion.4
  123.2 0.2 fusion.89
  123.7 0.3 convert_bitcast_fusion.2
  124.6 0.9 copy_dynamic-update-slice_fusion.2
  125.4 5.1 %copy.102 = bf16[8,16,8,2,512]{4,3,1,0,2:T(2,128)(2,1)} copy(bf16[8,16,8,2,512]{4,1,3,2,0:T(8,128)(2,1)} %bitcast.111) | data formatting | bytes 4194304 | tf_op jit(solution)/shard_map/reshape | solution.py:68
  130.5 3.6 %all-to-all-start.2 = ((bf16[8,16,8,2,512]{4,3,1,0,2:T(2,128)(2,1)}), bf16[8,16,8,2,512]{4,3,1,0,2:T(2,128)(2,1)S(1)}, u32[]{:S(2)}, u32[]{:S(2)}) async-start(bf16[8,16,8,2,512]{4,3,1,0,2:T(2,128)(2,1)} %copy.102), calls=%async_computation.2 | async-start | bytes 4194304 | tf_op jit(solution)/shard_map/all_to_all | solution.py:127
  134.3 1.3 convolution_bitcast_fusion
  135.6 2.0 copy.108
  137.7 79.9 %reduce-scatter.2.cloned.1.call-done = f32[16,8,128]{2,1,0:T(8,128)} async-done(((f32[128,8,128]{2,1,0:T(8,128)}), f32[16,8,128]{2,1,0:T(8,128)}) %reduce-scatter.2.cloned.1.call-update) | async-done | bytes 65552 | tf_op jit(solution)/shard_map/reduce_scatter | solution.py:141
  217.6 1.5 copy.109
  219.1 3.8 %copy.103 = bf16[8,16,8,2,512]{4,3,2,1,0:T(2,128)(2,1)} copy(bf16[8,16,8,2,512]{4,3,1,0,2:T(2,128)(2,1)S(1)} %all-to-all-done.2) | data formatting | bytes 4194304 | tf_op jit(solution)/shard_map/all_to_all | solution.py:127
  222.9 2.7 %reshape.322 = bf16[8,256,512]{2,1,0:T(8,128)(2,1)S(1)} reshape(bf16[8,16,8,2,512]{4,3,2,1,0:T(2,128)(2,1)} %copy.103) | data formatting | bytes 4194304 | tf_op jit(solution)/shard_map/reshape | solution.py:130
  225.7 7.3 %gather_fusion = bf16[1024,512]{1,0:T(8,128)(2,1)S(1)} fusion(bf16[8,256,512]{2,1,0:T(8,128)(2,1)S(1)} %reshape.322, s32[1024]{0:T(1024)S(1)} %get-tuple-element.138), kind=kCustom, calls=%fused_computation | custom fusion | bytes 2105344 | tf_op jit(solution)/shard_map/gather | solution.py:130
  233.0 0.3 slice_bitcast_fusion
  233.3 0.8 copy.128
  234.0 0.8 copy.129
  234.8 0.8 copy.130
  235.6 0.8 copy.131
  (118 shorter events, 10.4 us)
Async XLA Ops:
  7.2 18.3 %copy-start = (bf16[128,1024]{1,0:T(8,128)(2,1)S(1)}, bf16[128,1024]{1,0:T(8,128)(2,1)}, u32[]{:S(2)}) copy-start(bf16[128,1024]{1,0:T(8,128)(2,1)} %param.10) | copy-start | bytes 786436
  7.2 18.5 %copy-start.1 = (bf16[128,1024]{1,0:T(8,128)(2,1)S(1)}, bf16[128,1024]{1,0:T(8,128)(2,1)}, u32[]{:S(2)}) copy-start(bf16[128,1024]{1,0:T(8,128)(2,1)} %param.11) | copy-start | bytes 786436
  16.0 25.0 %all-to-all-start = ((s32[8,1,256]{2,1,0:T(1,128)}), s32[8,1,256]{2,1,0:T(1,128)S(1)}, u32[]{:S(2)}, u32[]{:S(2)}) async-start(s32[8,1,256]{2,1,0:T(1,128)} %reshape.359), calls=%async_computation | async-start | bytes 16384 | tf_op jit(solution)/shard_map/all_to_all | solution.py:118
  41.0 53.7 %all-to-all-start.1 = ((bf16[8,16,8,2,512]{4,3,1,0,2:T(2,128)(2,1)}), bf16[8,16,8,2,512]{4,3,1,0,2:T(2,128)(2,1)S(1)}, u32[]{:S(2)}, u32[]{:S(2)}) async-start(bf16[8,16,8,2,512]{4,3,1,0,2:T(2,128)(2,1)} %copy.97), calls=%async_computation.1 | async-start | bytes 4194304 | tf_op jit(solution)/shard_map/all_to_all | solution.py:115
  130.5 88.5 %all-to-all-start.2 = ((bf16[8,16,8,2,512]{4,3,1,0,2:T(2,128)(2,1)}), bf16[8,16,8,2,512]{4,3,1,0,2:T(2,128)(2,1)S(1)}, u32[]{:S(2)}, u32[]{:S(2)}) async-start(bf16[8,16,8,2,512]{4,3,1,0,2:T(2,128)(2,1)} %copy.102), calls=%async_computation.2 | async-start | bytes 4194304 | tf_op jit(solution)/shard_map/all_to_all | solution.py:127
  134.2 83.4 %reduce-scatter.2.cloned.1.call-start = ((), (), s32[]{:S(2)}) async-start(), calls=%async_computation.4 | async-start | bytes 589824 | tf_op jit(solution)/shard_map/reduce_scatter | solution.py:141
Sparse Core Ops, SparseCore 0:
  138.3 79.2 reduce-scatter.1
where the time goes:
time: 244 us; the launch traced here: 243 us
  waiting for transfers between devices  126 us (52%)
  local copies, waits for them, and re-layouts  68.5 us (28%)
  starting transfers between devices  16.9 us (7%)
  between operations  14.2 us (6%)
  matrix products  11.3 us (5%)
  other arithmetic  5.42 us (2%)
    reduce_scatter x1, waiting for transfers between devices, local(): lax.psum_scatter(jnp.einsum('htc,htd->chd', chosen.astype(jnp.float32), u...  79.9 us
    all_to_all x1, waiting for transfers between devices, local(): lax.all_to_all(send_rows.reshape(grid_rows), ('seq', 'help'), split_axis=...  46.4 us
    unnamed x14, local copies, waits for them, and re-layouts  15.7 us
    dynamic_slice x32, local copies, waits for them, and re-layouts, owner_work(): results = lax.map(one_head, (flat_rows, flat_pos)).reshape(arrived.shape)  9.65 us
    reshape x2, local copies, waits for them, and re-layouts, local(): send_rows.reshape(grid_rows)  7.49 us
    gather x1, local copies, waits for them, and re-layouts, local(): returned.reshape(local_heads, slot_total, 4 * depth)[head_index, flat_slot]  7.3 us
    all_to_all x1, starting transfers between devices, local(): lax.all_to_all(send_pos.reshape(grid_rows[:-1]), ('seq', 'help'), split_a...  7.25 us
    dynamic_update_slice x8, local copies, waits for them, and re-layouts, owner_work(): results = lax.map(one_head, (flat_rows, flat_pos)).reshape(arrived.shape)  6.92 us
  transfers between devices with their start and end apart: 4, of which 2 were waited for; matrix products, arithmetic and copies ran while one was open for 10% of the time, Pallas kernels for 0%

commit v1 on v0

--- a/solution.py
+++ b/solution.py
@@ -1,6 +1,10 @@
+import functools
+
 import jax
 import jax.numpy as jnp
 from jax import lax
+from jax.experimental import pallas as pl
+from jax.experimental.pallas import tpu as pltpu
 from jax.sharding import PartitionSpec as P
 
 BLK = 256
@@ -149,6 +153,299 @@
     return (pieces[0], pieces[1], pieces[2], pieces[3], centroid_sums)
 
 
+MASKED = -1e30
+
+
+def head_kernel(
+    seq_size,
+    help_size,
+    q_ref,
+    k_ref,
+    v_ref,
+    g_ref,
+    ids_ref,
+    slots_ref,
+    att_ref,
+    dq_ref,
+    dk_ref,
+    dv_ref,
+    sums_ref,
+    q_all,
+    k_all,
+    v_all,
+    g_all,
+    ids_all,
+    att_stage,
+    dq_stage,
+    dk_stage,
+    dv_stage,
+    sums_stage,
+    dk_total,
+    dv_total,
+    send_in,
+    recv_in,
+    send_out,
+    recv_out,
+):
+    devices = seq_size * help_size
+    tokens = q_ref.shape[0]
+    depth = q_all.shape[1]
+    clusters = slots_ref.shape[2]
+    owned = clusters // devices
+    me = lax.axis_index("seq") * help_size + lax.axis_index("help")
+
+    def place(index):
+        return {"seq": index // help_size, "help": lax.rem(index, help_size)}
+
+    def partner(step):
+        return lax.rem(me + step, devices)
+
+    def columns(index):
+        return pl.ds(pl.multiple_of(index * depth, depth), depth)
+
+    def rows(index):
+        return pl.ds(pl.multiple_of(index * tokens, tokens), tokens)
+
+    barrier = pltpu.get_barrier_semaphore()
+    for step in range(1, devices):
+        pl.semaphore_signal(
+            barrier, inc=1, device_id=place(partner(step)), device_id_type=pl.DeviceIdType.MESH
+        )
+
+    sources = (k_ref, q_ref, v_ref, g_ref)
+    landings = (k_all, q_all, v_all, g_all)
+
+    own_in = [
+        pltpu.make_async_copy(source.at[:, columns(me)], landing.at[rows(me)], send_in.at[0, item])
+        for item, (source, landing) in enumerate(zip(sources, landings))
+    ]
+    own_in.append(pltpu.make_async_copy(ids_ref.at[me], ids_all.at[me], send_in.at[0, 4]))
+    for copy in own_in:
+        copy.start()
+    pl.semaphore_wait(barrier, devices - 1)
+
+    def inbound(step):
+        target = partner(step)
+        copies = [
+            pltpu.make_async_remote_copy(
+                src_ref=ids_ref.at[target],
+                dst_ref=ids_all.at[me],
+                send_sem=send_in.at[step, 4],
+                recv_sem=recv_in.at[step, 4],
+                device_id=place(target),
+                device_id_type=pl.DeviceIdType.MESH,
+            )
+        ]
+        for item, (source, landing) in enumerate(zip(sources, landings)):
+            copies.append(
+                pltpu.make_async_remote_copy(
+                    src_ref=source.at[:, columns(target)],
+                    dst_ref=landing.at[rows(me)],
+                    send_sem=send_in.at[step, item],
+                    recv_sem=recv_in.at[step, item],
+                    device_id=place(target),
+                    device_id_type=pl.DeviceIdType.MESH,
+                )
+            )
+        return copies
+
+    incoming = [inbound(step) for step in range(1, devices)]
+    for copies in incoming:
+        for copy in copies:
+            copy.start()
+    for copy in own_in:
+        copy.wait()
+    for copies in incoming:
+        for copy in copies:
+            copy.wait()
+
+    stages = (att_stage, dq_stage, dk_stage, dv_stage)
+    results = (att_ref, dq_ref, dk_ref, dv_ref)
+
+    def outbound(target):
+        return [
+            pltpu.make_async_remote_copy(
+                src_ref=stage.at[rows(target)],
+                dst_ref=result.at[:, columns(me)],
+                send_sem=send_out.at[target, item],
+                recv_sem=recv_out.at[me, item],
+                device_id=place(target),
+                device_id_type=pl.DeviceIdType.MESH,
+            )
+            for item, (stage, result) in enumerate(zip(stages, results))
+        ]
+
+    def own_out(target):
+        return [
+            pltpu.make_async_copy(
+                stage.at[rows(target)], result.at[:, columns(target)], send_out.at[target, item]
+            )
+            for item, (stage, result) in enumerate(zip(stages, results))
+        ]
+
+    labels = [ids_all[index].astype(jnp.float32) for index in range(devices)]
+    label_row = jnp.concatenate(labels, axis=1)
+    label_columns = [
+        jnp.transpose(jnp.broadcast_to(label, (tokens, tokens)))[:, :1] for label in labels
+    ]
+
+    scale = depth ** (-0.5)
+    group = 2 if devices % 2 == 0 else 1
+    block = group * tokens
+    blocks = devices // group
+    dk_total[...] = jnp.zeros_like(dk_total)
+    dv_total[...] = jnp.zeros_like(dv_total)
+    earlier = lax.broadcasted_iota(jnp.int32, (block, block), 1) <= lax.broadcasted_iota(
+        jnp.int32, (block, block), 0
+    )
+    for index in reversed(range(blocks)):
+        low, high = index * block, (index + 1) * block
+        query, grad = q_all[low:high], g_all[low:high]
+        keys, values = k_all[:high], v_all[:high]
+        label_column = jnp.concatenate(
+            label_columns[index * group : (index + 1) * group], axis=0
+        )
+        allowed = label_column == label_row[:, :high]
+        near = allowed[:, low:] & earlier
+        allowed = near if low == 0 else jnp.concatenate([allowed[:, :low], near], axis=1)
+        scores = (
+            lax.dot_general(
+                query, keys, (((1,), (1,)), ((), ())), preferred_element_type=jnp.float32
+            )
+            * scale
+        )
+        scores = jnp.where(allowed, scores, MASKED)
+        peak = jnp.max(scores, axis=1, keepdims=True)
+        weights = jnp.exp(scores - peak)
+        weights = weights * (1.0 / jnp.sum(weights, axis=1, keepdims=True))
+        weights_low = weights.astype(jnp.bfloat16)
+        context = jnp.dot(weights_low, values, preferred_element_type=jnp.float32)
+        dv_total[:high] += lax.dot_general(
+            weights_low, grad, (((0,), (0,)), ((), ())), preferred_element_type=jnp.float32
+        )
+        grad_weights = lax.dot_general(
+            grad, values, (((1,), (1,)), ((), ())), preferred_element_type=jnp.float32
+        )
+        delta = jnp.sum(grad.astype(jnp.float32) * context, axis=1, keepdims=True)
+        grad_scores = (weights * (grad_weights - delta)).astype(jnp.bfloat16)
+        att_stage[low:high] = context.astype(jnp.bfloat16)
+        dq_stage[low:high] = (
+            jnp.dot(grad_scores, keys, preferred_element_type=jnp.float32) * scale
+        ).astype(jnp.bfloat16)
+        dk_total[:high] += lax.dot_general(
+            grad_scores, query, (((0,), (0,)), ((), ())), preferred_element_type=jnp.float32
+        )
+        dk_stage[low:high] = (dk_total[low:high] * scale).astype(jnp.bfloat16)
+        dv_stage[low:high] = dv_total[low:high].astype(jnp.bfloat16)
+        for target in range(index * group, (index + 1) * group):
+
+            @pl.when(me != target)
+            def _():
+                for copy in outbound(target):
+                    copy.start()
+
+            @pl.when(me == target)
+            def _():
+                for copy in own_out(target):
+                    copy.start()
+
+    key_float = k_all[...].astype(jnp.float32)
+    spread = jnp.mean(key_float * key_float, axis=1, keepdims=True)
+    units = key_float * (lax.rsqrt(spread + 1e-06) * scale)
+    units_high = units.astype(jnp.bfloat16)
+    units_rest = (units - units_high.astype(jnp.float32)).astype(jnp.bfloat16)
+    numbers = lax.broadcasted_iota(jnp.int32, (clusters, 1), 0)
+    named = (numbers.astype(jnp.float32) == label_row).astype(jnp.bfloat16)
+    owner_of = (numbers == slots_ref[me]).astype(jnp.bfloat16)
+    chosen = jnp.dot(owner_of, named, preferred_element_type=jnp.float32).astype(jnp.bfloat16)
+    sums_stage[...] = jnp.dot(
+        chosen, units_high, preferred_element_type=jnp.float32
+    ) + jnp.dot(chosen, units_rest, preferred_element_type=jnp.float32)
+
+    def slots_at(target):
+        return pl.ds(pl.multiple_of(target * owned, owned), owned)
+
+    def sums_out(step):
+        target = partner(step)
+        return pltpu.make_async_remote_copy(
+            src_ref=sums_stage.at[slots_at(target)],
+            dst_ref=sums_ref.at[me],
+            send_sem=send_in.at[step, 5],
+            recv_sem=recv_in.at[step, 5],
+            device_id=place(target),
+            device_id_type=pl.DeviceIdType.MESH,
+        )
+
+    sums_copies = [sums_out(step) for step in range(1, devices)]
+    sums_copies.append(
+        pltpu.make_async_copy(sums_stage.at[slots_at(me)], sums_ref.at[me], send_in.at[0, 5])
+    )
+    for copy in sums_copies:
+        copy.start()
+
+    for target in range(devices):
+
+        @pl.when(me != target)
+        def _():
+            for item, (stage, result) in enumerate(zip(stages, results)):
+                copy = pltpu.make_async_remote_copy(
+                    src_ref=stage.at[rows(target)],
+                    dst_ref=result.at[:, columns(target)],
+                    send_sem=send_out.at[target, item],
+                    recv_sem=recv_out.at[target, item],
+                    device_id=place(target),
+                    device_id_type=pl.DeviceIdType.MESH,
+                )
+                copy.wait_send()
+                copy.wait_recv()
+
+        @pl.when(me == target)
+        def _():
+            for copy in own_out(target):
+                copy.wait()
+
+    for copy in sums_copies:
+        copy.wait()
+
+
+def routed_by_head(query_rows, key_rows, value_rows, out_grad, cluster_ids, cluster_slots):
+    token_count, width = query_rows.shape
+    local_heads, cluster_total = cluster_slots.shape
+    depth = width // local_heads
+    seq_size, help_size = lax.axis_size("seq"), lax.axis_size("help")
+    devices = seq_size * help_size
+    if devices != local_heads:
+        return local(query_rows, key_rows, value_rows, out_grad, cluster_ids, cluster_slots)
+    total = devices * token_count
+    low = jnp.bfloat16
+    full = (total, depth)
+    return pl.pallas_call(
+        functools.partial(head_kernel, seq_size, help_size),
+        out_shape=[jax.ShapeDtypeStruct((token_count, width), low)] * 4
+        + [jax.ShapeDtypeStruct((local_heads, cluster_total // devices, depth), jnp.float32)],
+        in_specs=[pl.BlockSpec(memory_space=pl.ANY)] * 4
+        + [pl.BlockSpec(memory_space=pltpu.VMEM)] * 2,
+        out_specs=[pl.BlockSpec(memory_space=pl.ANY)] * 5,
+        scratch_shapes=[pltpu.VMEM(full, low)] * 4
+        + [pltpu.VMEM((devices, 1, token_count), jnp.int32)]
+        + [pltpu.VMEM(full, low)] * 4
+        + [pltpu.VMEM((cluster_total, depth), jnp.float32)]
+        + [pltpu.VMEM(full, jnp.float32)] * 2
+        + [pltpu.SemaphoreType.DMA((devices, 6))] * 2
+        + [pltpu.SemaphoreType.DMA((devices, 4))] * 2,
+        compiler_params=pltpu.CompilerParams(
+            collective_id=0, has_side_effects=True, vmem_limit_bytes=48 * 1024 * 1024
+        ),
+    )(
+        query_rows,
+        key_rows,
+        value_rows,
+        out_grad,
+        cluster_ids.reshape(local_heads, 1, token_count),
+        cluster_slots.reshape(local_heads, 1, cluster_total),
+    )
+
+
 def solution(mesh):
     in_specs = (
         P(("groups", "seq", "help"), "head"),
@@ -165,4 +462,4 @@
         P(("groups", "seq", "help"), "head"),
         P(("groups", "head"), ("seq", "help"), None),
     )
-    return jax.shard_map(local, mesh=mesh, in_specs=in_specs, out_specs=out_specs, check_vma=False)
+    return jax.shard_map(routed_by_head, mesh=mesh, in_specs=in_specs, out_specs=out_specs, check_vma=False)

time: 244 us -> 75.5 us (0.31)
  waiting for transfers between devices: 126 us -> 0 us
  Pallas kernels: 0 us -> 65.9 us
  local copies, waits for them, and re-layouts: 68.5 us -> 8.6 us
  starting transfers between devices: 16.9 us -> 0 us
  between operations: 14.2 us -> 0.66 us
  matrix products: 11.3 us -> 0 us
  other arithmetic: 5.42 us -> 0 us
    reduce_scatter x1 -> x0, waiting for transfers between devices: 79.9 us -> none  [local(): lax.psum_scatter(jnp.einsum('htc,htd->chd', chosen.astype(jnp.float32), u...]
    pallas_call x0 -> x1, Pallas kernels: none -> 65.9 us  [routed_by_head(): pl.pallas_call(functools.partial(head_kernel, seq_size, help_size), out_s...]
    all_to_all x3 -> x0, waiting for transfers between devices: 46.4 us -> none  [the longest x1 46.4 us: local(): lax.all_to_all(send_rows.reshape(grid_rows), ('seq', 'help'), split_axis=...]
    reshape x10 -> x0, local copies, waits for them, and re-layouts: 19.4 us -> none  [the longest x2 7.49 us: local(): send_rows.reshape(grid_rows)]
    all_to_all x3 -> x0, starting transfers between devices: 16.9 us -> none  [the longest x1 7.25 us: local(): lax.all_to_all(send_pos.reshape(grid_rows[:-1]), ('seq', 'help'), split_a...]
    dynamic_slice x32 -> x0, local copies, waits for them, and re-layouts: 9.65 us -> none  [owner_work(): results = lax.map(one_head, (flat_rows, flat_pos)).reshape(arrived.shape)]
    dot_general x41 -> x0, matrix products: 9.42 us -> none  [the longest x8 2.48 us: cluster_attention(): jnp.dot(weights_low, value_part, preferred_element_type=jnp.float32)]
    gather x1 -> x0, local copies, waits for them, and re-layouts: 7.3 us -> none  [local(): returned.reshape(local_heads, slot_total, 4 * depth)[head_index, flat_slot]]
  transfers between devices with their start and end apart: 4 -> 0, of which waited for: 2 -> 0; matrix products, arithmetic and copies ran while one was open for 10% -> 0% of each run, Pallas kernels for 0% -> 0%
where the time goes in v1:
time: 75.5 us; the launch traced here: 75.2 us
  Pallas kernels  65.9 us (87%)
  local copies, waits for them, and re-layouts  8.6 us (11%)
    pallas_call x1, Pallas kernels, routed_by_head(): pl.pallas_call(functools.partial(head_kernel, seq_size, help_size), out_s...  65.9 us
    unnamed x17, local copies, waits for them, and re-layouts  8.6 us

profile of v1, /device:TPU:0, one launch (start us, length us, event | category | flops | bytes accessed | tf_op | source)
XLA Modules:
  0.0 75.2 jit_solution(10037971849858094390)
XLA Ops:
  0.6 0.0 copy-start
  0.6 0.9 %copy-done = bf16[128,1024]{1,0:T(8,128)(2,1)S(1)} copy-done((bf16[128,1024]{1,0:T(8,128)(2,1)S(1)}, bf16[128,1024]{1,0:T(8,128)(2,1)}, u32[]{:S(2)}) %copy-start) | copy-done | bytes 262168
  1.6 0.0 copy-start.1
  1.6 0.9 %copy-done.1 = bf16[128,1024]{1,0:T(8,128)(2,1)S(1)} copy-done((bf16[128,1024]{1,0:T(8,128)(2,1)S(1)}, bf16[128,1024]{1,0:T(8,128)(2,1)}, u32[]{:S(2)}) %copy-start.1) | copy-done | bytes 262168
  2.5 0.0 copy-start.2
  2.5 0.9 %copy-done.2 = bf16[128,1024]{1,0:T(8,128)(2,1)S(1)} copy-done((bf16[128,1024]{1,0:T(8,128)(2,1)S(1)}, bf16[128,1024]{1,0:T(8,128)(2,1)}, u32[]{:S(2)}) %copy-start.2) | copy-done | bytes 262168
  3.5 0.0 copy-start.3
  3.5 0.9 %copy-done.3 = bf16[128,1024]{1,0:T(8,128)(2,1)S(1)} copy-done((bf16[128,1024]{1,0:T(8,128)(2,1)S(1)}, bf16[128,1024]{1,0:T(8,128)(2,1)}, u32[]{:S(2)}) %copy-start.3) | copy-done | bytes 262168
  4.4 0.0 copy-start.4
  4.4 0.7 copy-done.4
  5.1 0.0 copy-start.5
  5.1 0.7 copy-done.5
  5.8 65.9 %shard_map.101 = (bf16[128,1024]{1,0:T(8,128)(2,1)S(1)}, bf16[128,1024]{1,0:T(8,128)(2,1)S(1)}, bf16[128,1024]{1,0:T(8,128)(2,1)S(1)}, bf16[128,1024]{1,0:T(8,128)(2,1)S(1)}, f32[8,16,128]{2,1,0:T(8,128)S(1)}) custom-call(bf16[128,1024]{1,0:T(8,128)(2,1)S(1)} %copy-done, bf16[128,1024]{1,0:T(8,128)(2,1)S(1)} %copy-done.1, bf16[128,1024]{1,0:T(8,128)(2,1)S(1)} %copy-done.2, ...), custom_call_target="tpu_custom_call" | custom-call | tf_op jit(solution)/shard_map/pallas_call | solution.py:422
  71.7 0.7 copy.16
  72.4 0.7 copy.17
  73.1 0.7 copy.18
  73.8 0.7 copy.19
  74.5 0.6 copy.20
Async XLA Ops:
  0.6 1.0 %copy-start = (bf16[128,1024]{1,0:T(8,128)(2,1)S(1)}, bf16[128,1024]{1,0:T(8,128)(2,1)}, u32[]{:S(2)}) copy-start(bf16[128,1024]{1,0:T(8,128)(2,1)} %q_ref.1) | copy-start | bytes 786436
  1.6 0.9 %copy-start.1 = (bf16[128,1024]{1,0:T(8,128)(2,1)S(1)}, bf16[128,1024]{1,0:T(8,128)(2,1)}, u32[]{:S(2)}) copy-start(bf16[128,1024]{1,0:T(8,128)(2,1)} %k_ref.1) | copy-start | bytes 786436
  2.5 0.9 %copy-start.2 = (bf16[128,1024]{1,0:T(8,128)(2,1)S(1)}, bf16[128,1024]{1,0:T(8,128)(2,1)}, u32[]{:S(2)}) copy-start(bf16[128,1024]{1,0:T(8,128)(2,1)} %v_ref.1) | copy-start | bytes 786436
  3.5 0.9 %copy-start.3 = (bf16[128,1024]{1,0:T(8,128)(2,1)S(1)}, bf16[128,1024]{1,0:T(8,128)(2,1)}, u32[]{:S(2)}) copy-start(bf16[128,1024]{1,0:T(8,128)(2,1)} %g_ref.1) | copy-start | bytes 786436
  4.4 0.7 copy-start.4
  5.1 0.7 copy-start.5

commit v2 on v0

--- a/solution.py
+++ b/solution.py
@@ -1,6 +1,10 @@
+import functools
+
 import jax
 import jax.numpy as jnp
 from jax import lax
+from jax.experimental import pallas as pl
+from jax.experimental.pallas import tpu as pltpu
 from jax.sharding import PartitionSpec as P
 
 BLK = 256
@@ -149,6 +153,427 @@
     return (pieces[0], pieces[1], pieces[2], pieces[3], centroid_sums)
 
 
+MASKED = -1e30
+
+
+def head_kernel(
+    seq_size,
+    help_size,
+    parts,
+    q_ref,
+    k_ref,
+    v_ref,
+    g_ref,
+    ids_ref,
+    slots_ref,
+    att_ref,
+    dq_ref,
+    dk_ref,
+    dv_ref,
+    dk_far_ref,
+    dv_far_ref,
+    sums_ref,
+    q_all,
+    k_all,
+    v_all,
+    g_all,
+    ids_all,
+    att_stage,
+    dq_stage,
+    dk_stage,
+    dv_stage,
+    sums_stage,
+    dk_total,
+    dv_total,
+    send_in,
+    recv_in,
+    send_ids,
+    recv_ids,
+    send_out,
+    recv_out,
+    send_sums,
+    recv_sums,
+):
+    devices = seq_size * help_size
+    owners = devices // parts
+    share, _, depth = q_all.shape
+    tokens = q_ref.shape[0]
+    clusters = slots_ref.shape[2]
+    owned = clusters // devices
+    me = lax.axis_index("seq") * help_size + lax.axis_index("help")
+    part = me // owners
+    rank = lax.rem(me, owners)
+
+    def place(index):
+        return {"seq": index // help_size, "help": lax.rem(index, help_size)}
+
+    def partner(step):
+        return lax.rem(me + step, devices)
+
+    def fellow(away, step):
+        return (part + away) * owners + lax.rem(rank + step, owners)
+
+    def columns(head):
+        return pl.ds(pl.multiple_of(head * depth, depth), depth)
+
+    def rows(index):
+        return pl.ds(pl.multiple_of(index * tokens, tokens), tokens)
+
+    def remote(source, landing, send_sem, recv_sem, target):
+        return pltpu.make_async_remote_copy(
+            src_ref=source,
+            dst_ref=landing,
+            send_sem=send_sem,
+            recv_sem=recv_sem,
+            device_id=place(target),
+            device_id_type=pl.DeviceIdType.MESH,
+        )
+
+    barrier = pltpu.get_barrier_semaphore()
+    for step in range(1, devices):
+        pl.semaphore_signal(
+            barrier, inc=1, device_id=place(partner(step)), device_id_type=pl.DeviceIdType.MESH
+        )
+
+    sources = (k_ref, v_ref, q_ref, g_ref)
+    landings = (k_all, v_all, q_all, g_all)
+
+    def head_in(item, inner, source, target):
+        return remote(
+            sources[item].at[:, columns(lax.rem(target, owners) * share + inner)],
+            landings[item].at[inner, rows(source)],
+            send_in.at[inner, target, item],
+            recv_in.at[inner, source, item],
+            target,
+        )
+
+    def ids_in(source, target):
+        first = lax.rem(target, owners) * share
+        return remote(
+            ids_ref.at[pl.ds(first, share)],
+            ids_all.at[source],
+            send_ids.at[target],
+            recv_ids.at[source],
+            target,
+        )
+
+    def own_in(item, inner):
+        return pltpu.make_async_copy(
+            sources[item].at[:, columns(rank * share + inner)],
+            landings[item].at[inner, rows(me)],
+            send_in.at[inner, me, item],
+        )
+
+    own_ids = pltpu.make_async_copy(
+        ids_ref.at[pl.ds(rank * share, share)], ids_all.at[me], send_ids.at[me]
+    )
+    own_ids.start()
+    for inner in range(share):
+        for item in range(4):
+            own_in(item, inner).start()
+    pl.semaphore_wait(barrier, devices - 1)
+
+    for away in range(1, parts):
+
+        @pl.when(part + away < parts)
+        def _():
+            for step in range(owners):
+                ids_in(me, fellow(away, step)).start()
+
+    for step in range(1, owners):
+        ids_in(me, fellow(0, step)).start()
+    for inner in range(share):
+        for away in range(1, parts):
+
+            @pl.when(part + away < parts)
+            def _():
+                for step in range(owners):
+                    for item in range(2):
+                        head_in(item, inner, me, fellow(away, step)).start()
+
+        for step in range(1, owners):
+            for item in range(4):
+                head_in(item, inner, me, fellow(0, step)).start()
+
+    stages = (att_stage, dq_stage, dk_stage, dv_stage)
+    results = (att_ref, dq_ref, dk_ref, dv_ref)
+    fars = (dk_far_ref, dv_far_ref)
+
+    def head_out(item, inner, owner, target):
+        return remote(
+            stages[item].at[inner, rows(target)],
+            results[item].at[:, columns(lax.rem(owner, owners) * share + inner)],
+            send_out.at[inner, target, item],
+            recv_out.at[inner, owner, item],
+            target,
+        )
+
+    def far_out(item, inner, owner, target):
+        return remote(
+            stages[2 + item].at[inner, rows(target)],
+            fars[item].at[:, columns(lax.rem(owner, owners) * share + inner)],
+            send_out.at[inner, target, 2 + item],
+            recv_out.at[inner, owner, 2 + item],
+            target,
+        )
+
+    def own_out(item, inner):
+        return pltpu.make_async_copy(
+            stages[item].at[inner, rows(me)],
+            results[item].at[:, columns(rank * share + inner)],
+            send_out.at[inner, me, item],
+        )
+
+    def sums_slice(target):
+        return pl.ds(pl.multiple_of(target * owned, owned), owned)
+
+    def sums_out(inner, owner, target):
+        return remote(
+            sums_stage.at[inner, sums_slice(target)],
+            sums_ref.at[lax.rem(owner, owners) * share + inner],
+            send_sums.at[inner, target],
+            recv_sums.at[inner, owner],
+            target,
+        )
+
+    def own_sums(inner):
+        return pltpu.make_async_copy(
+            sums_stage.at[inner, sums_slice(me)],
+            sums_ref.at[rank * share + inner],
+            send_sums.at[inner, me],
+        )
+
+    scale = depth ** (-0.5)
+    group = 2 if owners % 2 == 0 else 1
+    block = group * tokens
+    earlier = lax.broadcasted_iota(jnp.int32, (block, block), 1) <= lax.broadcasted_iota(
+        jnp.int32, (block, block), 0
+    )
+
+    def attend(inner, first, last, label_row, label_columns):
+        for index in reversed(range(first, last)):
+            low, high = index * block, (index + 1) * block
+            query, grad = q_all[inner, low:high], g_all[inner, low:high]
+            keys, values = k_all[inner, :high], v_all[inner, :high]
+            label_column = jnp.concatenate(
+                label_columns[index * group : (index + 1) * group], axis=0
+            )
+            allowed = label_column == label_row[:, :high]
+            near = allowed[:, low:] & earlier
+            allowed = near if low == 0 else jnp.concatenate([allowed[:, :low], near], axis=1)
+            scores = (
+                lax.dot_general(
+                    query, keys, (((1,), (1,)), ((), ())), preferred_element_type=jnp.float32
+                )
+                * scale
+            )
+            scores = jnp.where(allowed, scores, MASKED)
+            peak = jnp.max(scores, axis=1, keepdims=True)
+            weights = jnp.exp(scores - peak)
+            weights = weights * (1.0 / jnp.sum(weights, axis=1, keepdims=True))
+            weights_low = weights.astype(jnp.bfloat16)
+            context = jnp.dot(weights_low, values, preferred_element_type=jnp.float32)
+            grad_weights = lax.dot_general(
+                grad, values, (((1,), (1,)), ((), ())), preferred_element_type=jnp.float32
+            )
+            delta = jnp.sum(grad.astype(jnp.float32) * context, axis=1, keepdims=True)
+            grad_scores = (weights * (grad_weights - delta)).astype(jnp.bfloat16)
+            att_stage[inner, low:high] = context.astype(jnp.bfloat16)
+            dq_stage[inner, low:high] = (
+                jnp.dot(grad_scores, keys, preferred_element_type=jnp.float32) * scale
+            ).astype(jnp.bfloat16)
+            dv_more = lax.dot_general(
+                weights_low, grad, (((0,), (0,)), ((), ())), preferred_element_type=jnp.float32
+            )
+            dk_more = lax.dot_general(
+                grad_scores, query, (((0,), (0,)), ((), ())), preferred_element_type=jnp.float32
+            )
+            if index == last - 1:
+                dv_total[:high] = dv_more
+                dk_total[:high] = dk_more
+            else:
+                dv_total[:high] += dv_more
+                dk_total[:high] += dk_more
+        end = last * block
+        dk_stage[inner, :end] = (dk_total[:end] * scale).astype(jnp.bfloat16)
+        dv_stage[inner, :end] = dv_total[:end].astype(jnp.bfloat16)
+
+    def key_sums(inner, label_row):
+        key_float = k_all[inner].astype(jnp.float32)
+        spread = jnp.mean(key_float * key_float, axis=1, keepdims=True)
+        units = key_float * (lax.rsqrt(spread + 1e-06) * scale)
+        units_high = units.astype(jnp.bfloat16)
+        units_rest = (units - units_high.astype(jnp.float32)).astype(jnp.bfloat16)
+        numbers = lax.broadcasted_iota(jnp.int32, (clusters, 1), 0)
+        named = (numbers.astype(jnp.float32) == label_row).astype(jnp.bfloat16)
+        owner_of = (numbers == slots_ref[rank * share + inner]).astype(jnp.bfloat16)
+        chosen = jnp.dot(owner_of, named, preferred_element_type=jnp.float32).astype(jnp.bfloat16)
+        sums_stage[inner] = jnp.dot(
+            chosen, units_high, preferred_element_type=jnp.float32
+        ) + jnp.dot(chosen, units_rest, preferred_element_type=jnp.float32)
+
+    own_ids.wait()
+    for step in range(1, owners):
+        ids_in(fellow(0, step), me).wait_recv()
+
+    for mine in range(parts):
+
+        @pl.when(part == mine)
+        def _():
+            first, last = mine * owners // group, (mine + 1) * owners // group
+            before = mine * owners
+            for source in range(before):
+                ids_in(source, me).wait_recv()
+            for inner in range(share):
+                labels = [
+                    ids_all[index, inner].astype(jnp.float32) for index in range(before + owners)
+                ]
+                label_row = jnp.concatenate(labels, axis=1)
+                label_columns = [
+                    jnp.transpose(jnp.broadcast_to(label, (tokens, tokens)))[:, :1]
+                    for label in labels
+                ]
+                for item in range(4):
+                    own_in(item, inner).wait()
+                    for step in range(1, owners):
+                        head_in(item, inner, fellow(0, step), me).wait_recv()
+                for item in range(2):
+                    for source in range(before):
+                        head_in(item, inner, source, me).wait_recv()
+                attend(inner, first, last, label_row, label_columns)
+                for target in range(before):
+                    for item in range(2):
+                        far_out(item, inner, me, target).start()
+                for step in range(1, owners):
+                    for item in range(4):
+                        head_out(item, inner, me, fellow(0, step)).start()
+                for item in range(4):
+                    own_out(item, inner).start()
+                if mine == parts - 1:
+                    key_sums(inner, label_row)
+                    for step in range(1, devices):
+                        sums_out(inner, me, partner(step)).start()
+                    own_sums(inner).start()
+            for target in range(before):
+                for inner in range(share):
+                    for item in range(2):
+                        far_out(item, inner, me, target).wait_send()
+            for inner in range(share):
+                if mine == parts - 1:
+                    for step in range(1, devices):
+                        sums_out(inner, me, partner(step)).wait_send()
+                    own_sums(inner).wait()
+                    for step in range(1, owners):
+                        sums_out(inner, fellow(0, step), me).wait_recv()
+                else:
+                    for step in range(owners):
+                        sums_out(inner, (parts - 1) * owners + step, me).wait_recv()
+
+    for away in range(1, parts):
+
+        @pl.when(part + away < parts)
+        def _():
+            for step in range(owners):
+                ids_in(me, fellow(away, step)).wait_send()
+                for inner in range(share):
+                    for item in range(2):
+                        head_in(item, inner, me, fellow(away, step)).wait_send()
+                        far_out(item, inner, fellow(away, step), me).wait_recv()
+
+    for step in range(1, owners):
+        ids_in(me, fellow(0, step)).wait_send()
+        for inner in range(share):
+            for item in range(4):
+                head_in(item, inner, me, fellow(0, step)).wait_send()
+                head_out(item, inner, me, fellow(0, step)).wait_send()
+                head_out(item, inner, fellow(0, step), me).wait_recv()
+    for inner in range(share):
+        for item in range(4):
+            own_out(item, inner).wait()
+
+
+def finish_kernel(
+    help_size,
+    owners,
+    parts,
+    att_ref,
+    dq_ref,
+    dk_ref,
+    dv_ref,
+    dk_far_ref,
+    dv_far_ref,
+    sums_ref,
+    att_out,
+    dq_out,
+    dk_out,
+    dv_out,
+    sums_out,
+):
+    me = lax.axis_index("seq") * help_size + lax.axis_index("help")
+    has_far = me // owners + 1 < parts
+    att_out[...] = att_ref[...]
+    dq_out[...] = dq_ref[...]
+    sums_out[...] = sums_ref[...]
+    for near, far, out in ((dk_ref, dk_far_ref, dk_out), (dv_ref, dv_far_ref, dv_out)):
+        more = jnp.where(has_far, far[...].astype(jnp.float32), 0.0)
+        out[...] = (near[...].astype(jnp.float32) + more).astype(out.dtype)
+
+
+def routed_by_head(query_rows, key_rows, value_rows, out_grad, cluster_ids, cluster_slots):
+    token_count, width = query_rows.shape
+    local_heads, cluster_total = cluster_slots.shape
+    depth = width // local_heads
+    seq_size, help_size = lax.axis_size("seq"), lax.axis_size("help")
+    devices = seq_size * help_size
+    parts = 2
+    owners = devices // parts
+    if devices != local_heads or seq_size % parts or token_count != depth:
+        return local(query_rows, key_rows, value_rows, out_grad, cluster_ids, cluster_slots)
+    share = local_heads // owners
+    total = devices * token_count
+    low = jnp.bfloat16
+    full = (share, total, depth)
+    sums_shape = jax.ShapeDtypeStruct(
+        (local_heads, cluster_total // devices, depth), jnp.float32
+    )
+    rows_shape = jax.ShapeDtypeStruct((token_count, width), low)
+    landed = pl.pallas_call(
+        functools.partial(head_kernel, seq_size, help_size, parts),
+        out_shape=[rows_shape] * 6 + [sums_shape],
+        in_specs=[pl.BlockSpec(memory_space=pltpu.HBM)] * 4
+        + [pl.BlockSpec(memory_space=pltpu.VMEM)] * 2,
+        out_specs=[pl.BlockSpec(memory_space=pl.ANY)] * 7,
+        scratch_shapes=[pltpu.VMEM(full, low)] * 4
+        + [pltpu.VMEM((devices, share, 1, token_count), jnp.int32)]
+        + [pltpu.VMEM(full, low)] * 4
+        + [pltpu.VMEM((share, cluster_total, depth), jnp.float32)]
+        + [pltpu.VMEM((total, depth), jnp.float32)] * 2
+        + [pltpu.SemaphoreType.DMA((share, devices, 4))] * 2
+        + [pltpu.SemaphoreType.DMA((devices,))] * 2
+        + [pltpu.SemaphoreType.DMA((share, devices, 4))] * 2
+        + [pltpu.SemaphoreType.DMA((share, devices))] * 2,
+        compiler_params=pltpu.CompilerParams(
+            collective_id=0, has_side_effects=True, vmem_limit_bytes=40 * 1024 * 1024
+        ),
+    )(
+        query_rows,
+        key_rows,
+        value_rows,
+        out_grad,
+        cluster_ids.reshape(local_heads, 1, token_count),
+        cluster_slots.reshape(local_heads, 1, cluster_total),
+    )
+    return tuple(
+        pl.pallas_call(
+            functools.partial(finish_kernel, help_size, owners, parts),
+            out_shape=[rows_shape] * 4 + [sums_shape],
+            in_specs=[pl.BlockSpec(memory_space=pltpu.VMEM)] * 7,
+            out_specs=[pl.BlockSpec(memory_space=pltpu.VMEM)] * 5,
+            compiler_params=pltpu.CompilerParams(vmem_limit_bytes=16 * 1024 * 1024),
+        )(*landed)
+    )
+
+
 def solution(mesh):
     in_specs = (
         P(("groups", "seq", "help"), "head"),
@@ -165,4 +590,4 @@
         P(("groups", "seq", "help"), "head"),
         P(("groups", "head"), ("seq", "help"), None),
     )
-    return jax.shard_map(local, mesh=mesh, in_specs=in_specs, out_specs=out_specs, check_vma=False)
+    return jax.shard_map(routed_by_head, mesh=mesh, in_specs=in_specs, out_specs=out_specs, check_vma=False)

time: 244 us -> 58.5 us (0.24)
  waiting for transfers between devices: 126 us -> 0 us
  local copies, waits for them, and re-layouts: 68.5 us -> 5.16 us
  Pallas kernels: 0 us -> 52.3 us
  starting transfers between devices: 16.9 us -> 0 us
  between operations: 14.2 us -> 0.65 us
  matrix products: 11.3 us -> 0 us
  other arithmetic: 5.42 us -> 0 us
    reduce_scatter x1 -> x0, waiting for transfers between devices: 79.9 us -> none  [local(): lax.psum_scatter(jnp.einsum('htc,htd->chd', chosen.astype(jnp.float32), u...]
    pallas_call x0 -> x2, Pallas kernels: none -> 52.3 us  [the longest x1 51.2 us: routed_by_head(): pl.pallas_call(functools.partial(head_kernel, seq_size, help_size, parts)...]
    all_to_all x3 -> x0, waiting for transfers between devices: 46.4 us -> none  [the longest x1 46.4 us: local(): lax.all_to_all(send_rows.reshape(grid_rows), ('seq', 'help'), split_axis=...]
    reshape x10 -> x0, local copies, waits for them, and re-layouts: 19.4 us -> none  [the longest x2 7.49 us: local(): send_rows.reshape(grid_rows)]
    all_to_all x3 -> x0, starting transfers between devices: 16.9 us -> none  [the longest x1 7.25 us: local(): lax.all_to_all(send_pos.reshape(grid_rows[:-1]), ('seq', 'help'), split_a...]
    unnamed x14 -> x12, local copies, waits for them, and re-layouts: 15.7 us -> 5.16 us
    dynamic_slice x32 -> x0, local copies, waits for them, and re-layouts: 9.65 us -> none  [owner_work(): results = lax.map(one_head, (flat_rows, flat_pos)).reshape(arrived.shape)]
    dot_general x41 -> x0, matrix products: 9.42 us -> none  [the longest x8 2.48 us: cluster_attention(): jnp.dot(weights_low, value_part, preferred_element_type=jnp.float32)]
  transfers between devices with their start and end apart: 4 -> 0, of which waited for: 2 -> 0; matrix products, arithmetic and copies ran while one was open for 10% -> 0% of each run, Pallas kernels for 0% -> 0%
where the time goes in v2:
time: 58.5 us; the launch traced here: 58.1 us
  Pallas kernels  52.3 us (89%)
  local copies, waits for them, and re-layouts  5.16 us (9%)
  between operations  0.65 us (1%)
    pallas_call x1, Pallas kernels, routed_by_head(): pl.pallas_call(functools.partial(head_kernel, seq_size, help_size, parts)...  51.2 us
    unnamed x12, local copies, waits for them, and re-layouts  5.16 us

profile of v2, /device:TPU:0, one launch (start us, length us, event | category | flops | bytes accessed | tf_op | source)
XLA Modules:
  0.0 58.1 jit_solution(8436527040971971571)
XLA Ops:
  0.6 0.0 copy-start
  0.6 0.9 %copy-done = bf16[128,1024]{1,0:T(8,128)(2,1)S(1)} copy-done((bf16[128,1024]{1,0:T(8,128)(2,1)S(1)}, bf16[128,1024]{1,0:T(8,128)(2,1)}, u32[]{:S(2)}) %copy-start) | copy-done | bytes 262168
  1.6 0.0 copy-start.1
  1.6 0.9 %copy-done.1 = bf16[128,1024]{1,0:T(8,128)(2,1)S(1)} copy-done((bf16[128,1024]{1,0:T(8,128)(2,1)S(1)}, bf16[128,1024]{1,0:T(8,128)(2,1)}, u32[]{:S(2)}) %copy-start.1) | copy-done | bytes 262168
  2.5 0.0 copy-start.2
  2.5 0.9 %copy-done.2 = bf16[128,1024]{1,0:T(8,128)(2,1)S(1)} copy-done((bf16[128,1024]{1,0:T(8,128)(2,1)S(1)}, bf16[128,1024]{1,0:T(8,128)(2,1)}, u32[]{:S(2)}) %copy-start.2) | copy-done | bytes 262168
  3.5 0.0 copy-start.3
  3.5 0.9 %copy-done.3 = bf16[128,1024]{1,0:T(8,128)(2,1)S(1)} copy-done((bf16[128,1024]{1,0:T(8,128)(2,1)S(1)}, bf16[128,1024]{1,0:T(8,128)(2,1)}, u32[]{:S(2)}) %copy-start.3) | copy-done | bytes 262168
  4.4 0.0 copy-start.4
  4.4 0.7 %copy-done.4 = s32[8,128,1]{1,2,0:T(1,128)S(1)} copy-done((s32[8,128,1]{1,2,0:T(1,128)S(1)}, s32[8,128,1]{1,2,0:T(1,128)}, u32[]{:S(2)}) %copy-start.4) | copy-done | bytes 4120
  5.1 0.0 copy-start.5
  5.1 0.7 %copy-done.5 = s32[8,128]{1,0:T(8,128)S(1)} copy-done((s32[8,128]{1,0:T(8,128)S(1)}, s32[8,128]{1,0:T(8,128)}, u32[]{:S(2)}) %copy-start.5) | copy-done | bytes 4120
  5.8 51.2 %shard_map.101 = (bf16[128,1024]{1,0:T(8,128)(2,1)S(1)}, bf16[128,1024]{1,0:T(8,128)(2,1)S(1)}, bf16[128,1024]{1,0:T(8,128)(2,1)S(1)}, bf16[128,1024]{1,0:T(8,12...) custom-call(bf16[128,1024]{1,0:T(8,128)(2,1)S(1)} %copy-done, ...), custom_call_target="tpu_custom_call" | custom-call | tf_op jit(solution)/shard_map/pallas_call | solution.py:540
  57.1 1.1 %shard_map.102 = (bf16[128,1024]{1,0:T(8,128)(2,1)}, bf16[128,1024]{1,0:T(8,128)(2,1)}, bf16[128,1024]{1,0:T(8,128)(2,1)}, bf16[128,1024]{1,0:T(8,128)(2,1)}, f32[8,16,128]{2,1,0:T(8,128)}) custom-call(bf16[128,1024]{1,0:T(8,128)(2,1)S(1)} %get-tuple-element.12.att_ref, bf16[128,1024]{1,0:T(8,128)(2,1)S(1)} %get-tuple-element.13.dq_ref, ...), custom_call_target="tpu_custom_call" | custom-call | tf_op jit(solution)/shard_map/pallas_call | solution.py:567
Async XLA Ops:
  0.6 1.0 %copy-start = (bf16[128,1024]{1,0:T(8,128)(2,1)S(1)}, bf16[128,1024]{1,0:T(8,128)(2,1)}, u32[]{:S(2)}) copy-start(bf16[128,1024]{1,0:T(8,128)(2,1)} %q_ref.1) | copy-start | bytes 786436
  1.6 0.9 %copy-start.1 = (bf16[128,1024]{1,0:T(8,128)(2,1)S(1)}, bf16[128,1024]{1,0:T(8,128)(2,1)}, u32[]{:S(2)}) copy-start(bf16[128,1024]{1,0:T(8,128)(2,1)} %k_ref.1) | copy-start | bytes 786436
  2.5 0.9 %copy-start.2 = (bf16[128,1024]{1,0:T(8,128)(2,1)S(1)}, bf16[128,1024]{1,0:T(8,128)(2,1)}, u32[]{:S(2)}) copy-start(bf16[128,1024]{1,0:T(8,128)(2,1)} %v_ref.1) | copy-start | bytes 786436
  3.5 0.9 %copy-start.3 = (bf16[128,1024]{1,0:T(8,128)(2,1)S(1)}, bf16[128,1024]{1,0:T(8,128)(2,1)}, u32[]{:S(2)}) copy-start(bf16[128,1024]{1,0:T(8,128)(2,1)} %g_ref.1) | copy-start | bytes 786436
  4.4 0.7 %copy-start.4 = (s32[8,128,1]{1,2,0:T(1,128)S(1)}, s32[8,128,1]{1,2,0:T(1,128)}, u32[]{:S(2)}) copy-start(s32[8,128,1]{1,2,0:T(1,128)} %param.10) | copy-start | bytes 12292
  5.1 0.7 %copy-start.5 = (s32[8,128]{1,0:T(8,128)S(1)}, s32[8,128]{1,0:T(8,128)}, u32[]{:S(2)}) copy-start(s32[8,128]{1,0:T(8,128)} %param.11) | copy-start | bytes 12292

commit v3 on v2

--- a/solution.py
+++ b/solution.py
@@ -553,7 +553,7 @@
         + [pltpu.SemaphoreType.DMA((share, devices, 4))] * 2
         + [pltpu.SemaphoreType.DMA((share, devices))] * 2,
         compiler_params=pltpu.CompilerParams(
-            collective_id=0, has_side_effects=True, vmem_limit_bytes=40 * 1024 * 1024
+            collective_id=0, has_side_effects=True, vmem_limit_bytes=60 * 1024 * 1024
         ),
     )(
         query_rows,
@@ -569,7 +569,7 @@
             out_shape=[rows_shape] * 4 + [sums_shape],
             in_specs=[pl.BlockSpec(memory_space=pltpu.VMEM)] * 7,
             out_specs=[pl.BlockSpec(memory_space=pltpu.VMEM)] * 5,
-            compiler_params=pltpu.CompilerParams(vmem_limit_bytes=16 * 1024 * 1024),
+            compiler_params=pltpu.CompilerParams(vmem_limit_bytes=60 * 1024 * 1024),
         )(*landed)
     )
 

time: 58.5 us -> 55.5 us (0.949)
  local copies, waits for them, and re-layouts: 5.16 us -> 0 us
  Pallas kernels: 52.3 us -> 54.6 us
    unnamed x12 -> x0, local copies, waits for them, and re-layouts: 5.16 us -> none
    pallas_call x1, Pallas kernels: 1.08 us -> 2.35 us  [routed_by_head(): pl.pallas_call(functools.partial(finish_kernel, help_size, owners, parts)...]
    pallas_call x1, Pallas kernels: 51.2 us -> 52.3 us  [routed_by_head(): pl.pallas_call(functools.partial(head_kernel, seq_size, help_size, parts)...]
where the time goes in v3:
time: 55.5 us; the launch traced here: 55.3 us
  Pallas kernels  54.6 us (98%)
  between operations  0.64 us (1%)
    pallas_call x1, Pallas kernels, routed_by_head(): pl.pallas_call(functools.partial(head_kernel, seq_size, help_size, parts)...  52.3 us
    pallas_call x1, Pallas kernels, routed_by_head(): pl.pallas_call(functools.partial(finish_kernel, help_size, owners, parts)...  2.35 us

profile of v3, /device:TPU:0, one launch (start us, length us, event | category | flops | bytes accessed | tf_op | source)
XLA Modules:
  0.0 55.3 jit_solution(9728562968691189168)
XLA Ops:
  0.6 52.3 %shard_map.101 = (bf16[128,1024]{1,0:T(8,128)(2,1)}, bf16[128,1024]{1,0:T(8,128)(2,1)}, bf16[128,1024]{1,0:T(8,128)(2,1)}, bf16[128,1024]{1,0:T(8,128)(2,1)}, bf...) custom-call(bf16[128,1024]{1,0:T(8,128)(2,1)} %q_ref.1, bf16[128,1024]{1,0:T(8,128)(2,1)} %k_ref.1, ...), custom_call_target="tpu_custom_call" | custom-call | tf_op jit(solution)/shard_map/pallas_call | solution.py:540
  52.9 2.4 %shard_map.102 = (bf16[128,1024]{1,0:T(8,128)(2,1)}, bf16[128,1024]{1,0:T(8,128)(2,1)}, bf16[128,1024]{1,0:T(8,128)(2,1)}, bf16[128,1024]{1,0:T(8,128)(2,1)}, f32[8,16,128]{2,1,0:T(8,128)}) custom-call(bf16[128,1024]{1,0:T(8,128)(2,1)} %get-tuple-element.12.att_ref, bf16[128,1024]{1,0:T(8,128)(2,1)} %get-tuple-element.13.dq_ref, ...), custom_call_target="tpu_custom_call" | custom-call | tf_op jit(solution)/shard_map/pallas_call | solution.py:567

commit v4 on v3

--- a/solution.py
+++ b/solution.py
@@ -441,6 +441,12 @@
                     for source in range(before):
                         head_in(item, inner, source, me).wait_recv()
                 attend(inner, first, last, label_row, label_columns)
+                if inner == 0:
+                    for away in range(1, parts - mine):
+                        for step in range(owners):
+                            for each in range(share):
+                                for item in range(2):
+                                    head_in(item, each, me, fellow(away, step)).wait_send()
                 for target in range(before):
                     for item in range(2):
                         far_out(item, inner, me, target).start()
@@ -477,7 +483,6 @@
                 ids_in(me, fellow(away, step)).wait_send()
                 for inner in range(share):
                     for item in range(2):
-                        head_in(item, inner, me, fellow(away, step)).wait_send()
                         far_out(item, inner, fellow(away, step), me).wait_recv()
 
     for step in range(1, owners):

time: 55.5 us -> 55.5 us (level)
  no operation moved by 1% of the time
where the time goes in v4:
time: 55.5 us; the launch traced here: 55.3 us
  Pallas kernels  54.6 us (98%)
  between operations  0.64 us (1%)
    pallas_call x1, Pallas kernels, routed_by_head(): pl.pallas_call(functools.partial(head_kernel, seq_size, help_size, parts)...  52.3 us
    pallas_call x1, Pallas kernels, routed_by_head(): pl.pallas_call(functools.partial(finish_kernel, help_size, owners, parts)...  2.35 us

profile of v4, /device:TPU:0, one launch (start us, length us, event | category | flops | bytes accessed | tf_op | source)
XLA Modules:
  0.0 55.3 jit_solution(12970395237300853175)
XLA Ops:
  0.6 52.3 %shard_map.101 = (bf16[128,1024]{1,0:T(8,128)(2,1)}, bf16[128,1024]{1,0:T(8,128)(2,1)}, bf16[128,1024]{1,0:T(8,128)(2,1)}, bf16[128,1024]{1,0:T(8,128)(2,1)}, bf...) custom-call(bf16[128,1024]{1,0:T(8,128)(2,1)} %q_ref.1, bf16[128,1024]{1,0:T(8,128)(2,1)} %k_ref.1, ...), custom_call_target="tpu_custom_call" | custom-call | tf_op jit(solution)/shard_map/pallas_call | solution.py:545
  52.9 2.4 %shard_map.102 = (bf16[128,1024]{1,0:T(8,128)(2,1)}, bf16[128,1024]{1,0:T(8,128)(2,1)}, bf16[128,1024]{1,0:T(8,128)(2,1)}, bf16[128,1024]{1,0:T(8,128)(2,1)}, f32[8,16,128]{2,1,0:T(8,128)}) custom-call(bf16[128,1024]{1,0:T(8,128)(2,1)} %get-tuple-element.12.att_ref, bf16[128,1024]{1,0:T(8,128)(2,1)} %get-tuple-element.13.dq_ref, ...), custom_call_target="tpu_custom_call" | custom-call | tf_op jit(solution)/shard_map/pallas_call | solution.py:572
